TPU v7x, 1024 devices: a whole 4x4x32 slice. The times are simulated.
1024 devices in a mesh: table: 32 (over z), col: 4 (over y_lo, core), rep: 8 (over y_hi, x).
Axes of the slice: x: 4, y: 4 (y_hi: 2, y_lo: 2; y = y_hi * 2 + y_lo), z: 32, core: 2. Of those that a mesh axis runs over, the one named last changes fastest.
Arguments:
- pooled: bfloat16 [4096, 512, 160], P(('table', 'col', 'rep')), may hold values from -6 to 6
- upstream: bfloat16 [4096, 512, 160], P(('table', 'col', 'rep')), may hold values from -6 to 6
- lengths: int32 [4096, 512], P(('table', 'col', 'rep')), may hold values from 1 to 32
- w_lcb: bfloat16 [512, 512], replicated, may hold values from -0.25 to 0.25
- projection: bfloat16 [64, 512], replicated, may hold values from -0.25 to 0.25
- w_fmb: bfloat16 [64, 160], replicated, may hold values from -0.0625 to 0.0625
- feature_order: int32 [512], replicated, may hold values from 0 to 511, each once
- col_layout: int32 [32, 4], replicated, may hold values from 0 to 3, each once within a row
Outputs:
- table_grads: float32 [512, 4096, 160], P('table', 'rep', 'col')
- grad_lcb: float32 [512, 512], replicated
- grad_fmb: float32 [64, 160], replicated
- grad_proj: float32 [64, 512], replicated
Inputs may be any that keep to these rules, and one draw needn't show every extreme that they name: `feature_order`: a permutation of the features. `col_layout`: each row is a permutation of the column shards.
All inputs are finite; a program needn't handle non-finite values. Where the computation divides by a largest or mean magnitude, that divisor is 1e-20 or more.
Results may differ from a plain program's by a relative error of at most 0.012.
Values may be sent and summed in bfloat16 or wider, within the bound.
A program may use at most 32 MiB of HBM per device.

v0:
```python
import jax
import jax.numpy as jnp
from jax import lax
from jax.sharding import PartitionSpec as P


def by_group(bundle):
    return (
        lax.all_to_all(bundle[0], "table", split_axis=1, concat_axis=0, tiled=True),
        lax.all_to_all(bundle[1], "table", split_axis=1, concat_axis=0, tiled=True),
    )


def by_column(bundle):
    return (
        lax.all_to_all(bundle[0], "col", split_axis=2, concat_axis=0, tiled=True),
        lax.all_to_all(bundle[1], "col", split_axis=2, concat_axis=0, tiled=True),
    )


def body(pooled, upstream, lengths, w_lcb, projection, w_fmb, feature_order, col_layout):
    samples, features, model_width = pooled.shape
    groups = lax.axis_size("table")
    col_count = lax.axis_size("col")
    group_rows = features // groups
    piece_width = model_width // col_count
    wide = jnp.float32
    compressed = jnp.einsum("kf,sfd->skd", projection, pooled, preferred_element_type=wide).astype(
        jnp.bfloat16
    )
    interact = jnp.einsum("sfd,skd->sfk", pooled, compressed, preferred_element_type=wide).astype(
        jnp.bfloat16
    )
    grad_interact = jnp.einsum("sfd,kd->sfk", upstream, w_fmb, preferred_element_type=wide).astype(
        jnp.bfloat16
    )
    grad_compressed = jnp.einsum(
        "sfk,sfd->skd", grad_interact, pooled, preferred_element_type=wide
    ).astype(jnp.bfloat16)
    grad_lcb = jnp.einsum("sfd,sgd->fg", upstream, pooled, preferred_element_type=wide)
    grad_fmb = jnp.einsum("sfk,sfd->kd", interact, upstream, preferred_element_type=wide)
    grad_proj = jnp.einsum("skd,sfd->kf", grad_compressed, pooled, preferred_element_type=wide)
    summed = lax.psum((grad_lcb, grad_fmb, grad_proj), ("table", "col", "rep"))
    grad_input = upstream.astype(wide) + jnp.einsum(
        "fg,sfd->sgd", w_lcb, upstream, preferred_element_type=wide
    )
    grad_input = grad_input + jnp.einsum(
        "sfk,skd->sfd", grad_interact, compressed, preferred_element_type=wide
    )
    grad_input = grad_input + jnp.einsum(
        "kf,skd->sfd", projection, grad_compressed, preferred_element_type=wide
    )
    averaged = grad_input / lengths.astype(wide)[:, :, None]
    row_scale = (jnp.max(jnp.abs(averaged), axis=2) + 1e-06).astype(jnp.bfloat16)
    quantized = (averaged / row_scale.astype(wide)[:, :, None]).astype(jnp.bfloat16)
    ordered = jnp.take(quantized, feature_order, axis=1)
    ordered_scale = jnp.take(row_scale, feature_order, axis=1)
    targets = jnp.arange(col_count, dtype=jnp.int32)
    routing = (col_layout[:, None, :] == targets[None, :, None]).astype(jnp.bfloat16)
    arranged = jnp.einsum(
        "sgfjc,gdj->sgfdc",
        ordered.reshape(samples, groups, group_rows, col_count, piece_width),
        routing,
        preferred_element_type=wide,
    ).astype(jnp.bfloat16)
    arranged = arranged.reshape(samples, features, model_width)
    spread = jnp.broadcast_to(ordered_scale[:, :, None], (samples, features, col_count))
    sectioned = by_group((arranged, spread))
    received, received_scale = by_column(sectioned)
    received = received.reshape(col_count, groups, samples, group_rows, piece_width)
    received = received.transpose(1, 0, 2, 3, 4).reshape(
        groups * col_count * samples, group_rows, piece_width
    )
    received_scale = received_scale.reshape(col_count, groups, samples, group_rows, 1)
    received_scale = received_scale.transpose(1, 0, 2, 3, 4).reshape(
        groups * col_count * samples, group_rows, 1
    )
    restored = received.astype(wide) * received_scale.astype(wide)
    out_lcb, out_fmb, out_proj = (summed[0], summed[1], summed[2])
    return (restored.transpose(1, 0, 2), out_lcb, out_fmb, out_proj)


def solution(mesh):
    placed = (
        P(("table", "col", "rep"), None, None),
        P(("table", "col", "rep"), None, None),
        P(("table", "col", "rep"), None),
        P(),
        P(),
        P(),
        P(),
        P(),
    )
    return jax.shard_map(
        body,
        mesh=mesh,
        in_specs=placed,
        out_specs=(P("table", "rep", "col"), P(), P(), P()),
        check_vma=False,
    )
```

profile of v0, /device:TPU:1, one launch (start us, length us, event | category | flops | bytes accessed | tf_op | source)
XLA Modules:
  0.0 1095.8 jit_solution(15601750148785263364)
XLA Ops:
  7.2 0.8 compare_select_fusion
  7.9 0.7 compare_and_fusion
  8.6 1.3 convolution_convert_fusion
  10.0 0.3 convolution_convert_fusion.2
  10.4 0.3 convolution_convert_fusion.3
  10.7 0.4 convolution_bitcast_fusion
  11.1 0.4 copy-done.1
  11.4 0.2 copy-done.2
  11.6 0.5 fusion.5
  12.1 0.2 copy-done.8
  12.3 0.4 abs_reduce_fusion
  12.7 0.6 convert_multiply_fusion
  13.3 0.2 copy.73
  13.5 1.3 gather_fusion.1
  15.0 0.6 broadcast_bitcast_fusion
  15.6 1.4 reshape.93
  17.0 29.3 %all-to-all-start.2 = ((bf16[32,2,128]{2,1,0:T(2,128)(2,1)}), bf16[32,2,128]{2,1,0:T(2,128)(2,1)S(1)}, u32[]{:S(2)}, u32[]{:S(2)}) async-start(bf16[32,2,128]{2,1,0:T(2,128)(2,1)} %reshape.93), calls=%async_computation.2 | async-start | bytes 32768 | tf_op jit(solution)/shard_map/all_to_all | solution.py:10
  46.3 1.4 broadcast_in_dim.34
  47.7 0.2 divide_convert_fusion
  47.9 0.7 copy.63
  48.6 2.5 gather_fusion
  51.1 0.1 copy.64
  51.3 2.0 gather.11
  53.3 2.9 convert_bitcast_fusion
  56.2 0.9 copy.81
  57.1 2.2 reshape.92
  59.3 8.2 all-to-all-done.2
  67.5 13.0 %all-to-all-start = ((bf16[4,512,160]{2,0,1:T(4,128)(2,1)}), bf16[4,512,160]{2,0,1:T(4,128)(2,1)S(1)}, u32[]{:S(2)}, u32[]{:S(2)}) async-start(bf16[4,512,160]{2,0,1:T(4,128)(2,1)} %reshape.92), calls=%async_computation | async-start | bytes 2097152 | tf_op jit(solution)/shard_map/all_to_all | solution.py:9
  80.5 1.1 reshape.94
  81.7 1.0 copy.82
  82.8 0.7 copy.76
  83.5 102.4 %all-to-all-done = bf16[4,512,160]{2,0,1:T(4,128)(2,1)S(1)} async-done(((bf16[4,512,160]{2,0,1:T(4,128)(2,1)}), bf16[4,512,160]{2,0,1:T(4,128)(2,1)S(1)}, u32[]{:S(2)}, u32[]{:S(2)}) %all-to-all-start) | async-done | bytes 655392 | tf_op jit(solution)/shard_map/all_to_all | solution.py:9
  185.9 4.0 all-to-all-start.3
  189.8 1.6 convolution_bitcast_fusion.2
  191.4 0.2 copy.68
  191.6 1.8 copy.69
  193.5 3.7 all-to-all-start.1
  197.2 0.9 convolution_bitcast_fusion.3
  198.1 0.5 fusion.8
  198.6 158.1 %psum.22 = f32[64,160]{1,0:T(8,128)} all-reduce(f32[64,160]{1,0:T(8,128)S(1)} %fusion.8), channel_id=1, replica_groups=mesh['table'=32,'col'=4,'rep'=8] {'table','col','rep'}, use_global_device_ids=true, to_apply=%region_2.0 | all-reduce | flops 10240 | bytes 81920 | tf_op jit(solution)/shard_map/psum | solution.py:43
  356.9 0.2 copy.70
  357.2 2.9 copy.71
  360.1 2.5 copy.72
  362.6 3.5 bitcast_multiply_fusion
  366.2 3.7 copy.79
  369.8 716.2 %all-reduce.3.cloned.1.call-done = (f32[512,512]{1,0:T(8,128)}, f32[64,512]{1,0:T(8,128)}) async-done(((f32[512,512]{1,0:T(8,128)}, f32[64,512]{1,0:T(8,128)}), (f32[512,512]{1,0:T(8,128)}, f32[64,512]{1,0:T(8,128)})) %all-reduce.3.cloned.1.call-update) | async-done | bytes 1179664 | tf_op jit(solution)/shard_map/psum | solution.py:43
  1086.0 2.3 copy.90
  1088.3 0.7 copy.91
  (36 shorter events, 0.7 us)
Async XLA Ops:
  7.2 2.8 copy-start
  7.2 3.1 copy-start.5
  8.6 6.2 copy-start.10
  10.3 1.1 copy-start.1
  10.3 1.2 copy-start.2
  10.7 1.6 copy-start.3
  11.6 0.7 copy-start.8
  13.3 1.5 copy-start.9
  14.9 32.8 %copy-start.7 = (f32[4,512]{1,0:T(4,128)S(1)}, f32[4,512]{1,0:T(4,128)}, u32[]{:S(2)}) copy-start(f32[4,512]{1,0:T(4,128)} %get-tuple-element.22) | copy-start | bytes 24580
  17.0 50.5 %all-to-all-start.2 = ((bf16[32,2,128]{2,1,0:T(2,128)(2,1)}), bf16[32,2,128]{2,1,0:T(2,128)(2,1)S(1)}, u32[]{:S(2)}, u32[]{:S(2)}) async-start(bf16[32,2,128]{2,1,0:T(2,128)(2,1)} %reshape.93), calls=%async_computation.2 | async-start | bytes 32768 | tf_op jit(solution)/shard_map/all_to_all | solution.py:10
  51.2 2.0 copy-start.12
  51.2 2.1 copy-start.11
  67.5 118.3 %all-to-all-start = ((bf16[4,512,160]{2,0,1:T(4,128)(2,1)}), bf16[4,512,160]{2,0,1:T(4,128)(2,1)S(1)}, u32[]{:S(2)}, u32[]{:S(2)}) async-start(bf16[4,512,160]{2,0,1:T(4,128)(2,1)} %reshape.92), calls=%async_computation | async-start | bytes 2097152 | tf_op jit(solution)/shard_map/all_to_all | solution.py:9
  185.9 7.6 all-to-all-start.3
  193.5 163.4 %all-to-all-start.1 = ((bf16[128,16,160]{0,1,2:T(8,128)(2,1)}), bf16[128,16,160]{0,1,2:T(8,128)(2,1)S(1)}, u32[]{:S(2)}, u32[]{:S(2)}) async-start(bf16[128,16,160]{0,1,2:T(8,128)(2,1)} %copy.69), calls=%async_computation.1 | async-start | bytes 1310720 | tf_op jit(solution)/shard_map/all_to_all | solution.py:16
  197.1 1.0 copy-start.4
  197.1 888.9 %all-reduce.3.cloned.1.call-start = ((), (), s32[]{:S(2)}) async-start(), calls=%async_computation.4 | async-start | bytes 2359296 | tf_op jit(solution)/shard_map/psum | solution.py:43
  1086.0 2.3 copy-start.6
Sparse Core Ops, SparseCore 0:
  204.0 881.9 all-reduce.2
where the time goes:
time: 1100 us
  waiting for transfers between devices  827 us (75%)
  blocking collectives  158 us (14%)
  starting transfers between devices  49.9 us (5%)
  local copies, waits for them, and re-layouts  31.5 us (3%)
  between operations  14.3 us (1%)
    psum x1, waiting for transfers between devices, body(): summed = lax.psum((grad_lcb, grad_fmb, grad_proj), ('table', 'col', 'rep'))  716 us
    psum x1, blocking collectives, body(): summed = lax.psum((grad_lcb, grad_fmb, grad_proj), ('table', 'col', 'rep'))  158 us
    all_to_all x1, waiting for transfers between devices, by_group(): lax.all_to_all(bundle[0], 'table', split_axis=1, concat_axis=0, tiled=True)  102 us
    all_to_all x1, starting transfers between devices, by_group(): lax.all_to_all(bundle[1], 'table', split_axis=1, concat_axis=0, tiled=True)  29.3 us
  transfers between devices with their start and end apart: 5, of which 3 were waited for; matrix products, arithmetic and copies ran while one was open for 3% of the time, Pallas kernels for 0%

commit v1 on v0

v1 whole, which is shorter than its diff:
```python
import jax
import jax.numpy as jnp
from jax import lax
from jax.experimental import pallas as pl
from jax.experimental.pallas import tpu as pltpu
from jax.sharding import PartitionSpec as P

MESH = pl.DeviceIdType.MESH
WIDE = jnp.float32
HALF = jnp.bfloat16
S = 4
F = 512
D = 160
K = 64
PIECE = 40
ROWS = 16
X = 640
NT = 32
NX = 32
BLOCK = 8
CHUNKS = 16
DEEP = 3
OWNERS = 5
APART = 6


def nn(a, b):
    return lax.dot_general(a, b, (((1,), (0,)), ((), ())), preferred_element_type=WIDE)


def nt(a, b):
    return lax.dot_general(a, b, (((1,), (1,)), ((), ())), preferred_element_type=WIDE)


def tn(a, b):
    return lax.dot_general(a, b, (((0,), (0,)), ((), ())), preferred_element_type=WIDE)


def one_hot(mask):
    return jnp.where(mask, 1.0, 0.0).astype(HALF)


def iota(shape, dim):
    return lax.broadcasted_iota(jnp.int32, shape, dim)


def kernel(
    x_ref, g_ref, len_ref, lcb_ref, proj_ref, fmb_ref, order_ref, lay_ref,
    out_ref, gw_ref,
    rst, wide, send, zbuf, msend, mrecv, ct, gct, git, part, wbuf, mine, zred, tiles, full, px,
    zs, zr, ms, mr, ws, wr, rs, rr, os, og, fs, fr,
):
    t = lax.axis_index("table")
    c = lax.axis_index("col")
    r = lax.axis_index("rep")
    me = c * 8 + r
    block = t // BLOCK
    within = lax.rem(t, BLOCK)

    def plane(k):
        return {"col": k // 8, "rep": lax.rem(k, 8)}

    def remote(src, dst, ss, rsem, device):
        return pltpu.make_async_remote_copy(
            src_ref=src, dst_ref=dst, send_sem=ss, recv_sem=rsem, device_id=device, device_id_type=MESH
        )

    def done(ref, sem):
        pltpu.make_async_copy(ref, ref, sem).wait()

    barrier = pltpu.get_barrier_semaphore()

    @pl.loop(1, NT)
    def _(d):
        pl.semaphore_signal(barrier, inc=1, device_id={"table": lax.rem(t + d, NT)}, device_id_type=MESH)

    @pl.loop(1, NX)
    def _(d):
        pl.semaphore_signal(barrier, inc=1, device_id=plane(lax.rem(me + d, NX)), device_id_type=MESH)

    proj = proj_ref[...]
    ct[...] = nt(x_ref[...], proj).astype(HALF)
    for i in range(S):
        rows = pl.ds(i * D, D)
        git[i] = nn(fmb_ref[...], g_ref[rows, :]).astype(HALF)
        gct[rows, :] = nt(x_ref[rows, :], git[i]).astype(HALF)
    for i in range(S):
        rows = pl.ds(i * D, D)
        g = g_ref[rows, :]
        grad = g.astype(WIDE) + nn(g, lcb_ref[...])
        grad = grad + nn(ct[rows, :], git[i])
        grad = grad + nn(gct[rows, :], proj)
        averaged = grad * (1.0 / len_ref[pl.ds(i, 1), :].astype(WIDE))
        largest = jnp.max(jnp.abs(averaged), axis=0, keepdims=True)
        scale = (largest + 1e-06).astype(HALF).astype(WIDE)
        quantized = (averaged * (1.0 / scale)).astype(HALF)
        rst[rows, :] = (quantized.astype(WIDE) * scale).astype(HALF)

    into = one_hot(iota((F, F), 0) == order_ref[...])
    for i in range(S):
        ordered = nn(rst[pl.ds(i * D, D), :], into)
        for j in range(4):
            for gb in range(4):
                wide[gb, pl.ds(i * 4 + j, PIECE, stride=ROWS), :] = ordered[
                    j * PIECE : (j + 1) * PIECE, gb * 128 : (gb + 1) * 128
                ]

    lane_block = iota((ROWS, 128), 1) // 16
    for eb in range(5):
        for gb in range(4):
            turned = []
            for e in range(8):
                tile = wide[gb, pl.ds((eb * 8 + e) * ROWS, ROWS), :]
                turned.append(pltpu.roll(tile, 16 * e, 1) if e else tile)
            for g in range(8):
                mixed = turned[0]
                for e in range(1, 8):
                    mixed = jnp.where(lane_block == (g + e) % 8, turned[e], mixed)
                send[gb * 8 + g, :, pl.ds(eb * 128, 128)] = mixed.astype(HALF)
    zbuf[t] = send[t]

    def along(m):
        side = m - 8
        q = jnp.where(m < 8, block + 2, jnp.where(m < 24, block + 1 + 2 * lax.rem(side, 2), block))
        d = jnp.where(m < 8, m, jnp.where(m < 24, side // 2, m - 23))
        return lax.rem(q, 4) * BLOCK + lax.rem(within + d, BLOCK)

    def start(m, q):
        p = along(m)
        remote(send.at[p], zbuf.at[t], zs.at[q], zr.at[block], {"table": p}).start()

    def issue(first, last):
        @pl.loop(first, last)
        def _(q):
            @pl.when(q >= DEEP)
            def _():
                done(send.at[pl.ds(0, 2)], zs.at[q - DEEP])

            start(2 * q, q)

            @pl.when(q < CHUNKS - 1)
            def _():
                start(2 * q + 1, q)

    pl.semaphore_wait(barrier, NT + NX - 2)
    issue(0, DEEP)

    fmb_part = jnp.zeros((D, K), WIDE)
    for i in range(S):
        rows = pl.ds(i * D, D)
        interact = tn(ct[rows, :], x_ref[rows, :]).astype(HALF)
        fmb_part = fmb_part + nt(g_ref[rows, :], interact)
    part[:, pl.ds(0, F)] = tn(g_ref[...], x_ref[...])
    proj_part = tn(x_ref[...], gct[...])
    pad = jnp.zeros((F - D, K), WIDE)
    part[:, pl.ds(F, 128)] = jnp.concatenate([proj_part, jnp.concatenate([fmb_part, pad], axis=0)], axis=1)

    @pl.loop(1, NX)
    def _(d):
        k = lax.rem(me + d, NX)
        rows = pl.ds(pl.multiple_of(k * ROWS, ROWS), ROWS)
        remote(part.at[rows, :], wbuf.at[me], ws, wr, plane(k)).start()

    wbuf[me] = part[pl.ds(pl.multiple_of(me * ROWS, ROWS), ROWS), :]

    e = iota((PIECE, X), 0)
    place = (e // 8) * 128 + lax.rem(lax.rem(e, 8) + lax.rem(t, 8), 8) * 16
    for h in range(ROWS):
        px[pl.ds(h * PIECE, PIECE), :] = one_hot(iota((PIECE, X), 1) == place + h)
    a = iota((128, 128), 0)
    b = iota((128, 128), 1)
    j = b % 4
    owner = jnp.where(
        j == 0, lay_ref[t, 0], jnp.where(j == 1, lay_ref[t, 1], jnp.where(j == 2, lay_ref[t, 2], lay_ref[t, 3]))
    )
    by_column = one_hot((a % 32 == b // 4) & (owner == a // 32))
    by_sample = one_hot(b == ((a // 4) % 4) * 32 + (a // 16) * 4 + a % 4)

    issue(DEEP, 9)

    done(wbuf.at[pl.ds(0, NX - 1)], wr)
    total = wbuf[0]
    for k in range(1, NX):
        total = total + wbuf[k]
    for o in range(OWNERS):
        mine[o] = total[:, o * 128 : (o + 1) * 128]
    turn = lax.rem(t - me + NT, NT)
    owns = (lax.rem(turn, APART) == 0) & (turn < OWNERS * APART)
    index = jnp.minimum(turn // APART, OWNERS - 1)

    for o in range(OWNERS):
        to = lax.rem(me + o * APART, NT)

        @pl.when(to != t)
        def _():
            remote(mine.at[o], zred.at[t], rs, rr, {"table": to}).start()

    zred[t] = mine[index]

    def batch(s):
        return lax.rem(block + s, 4)

    def gather(s, count):
        q = batch(s)
        done(zbuf.at[pl.ds(0, count)], zr.at[q])
        got = zbuf[pl.ds(pl.multiple_of(q * BLOCK, BLOCK), BLOCK)].reshape(128, X)
        msend[q] = nn(by_column, got).astype(HALF).reshape(4, 32, X)
        for d in range(1, 4):
            k = lax.rem(c + d, 4)
            remote(msend.at[q, k], mrecv.at[q, c], ms.at[q], mr.at[q], {"col": k}).start()
        mrecv[q, c] = msend[q, c]

    def finish(s):
        q = batch(s)
        done(mrecv.at[q, pl.ds(0, 3)], mr.at[q])
        got = nn(by_sample, mrecv[q].reshape(128, X)).astype(HALF)
        out_ref[:, pl.ds(pl.multiple_of(q * 128, 128), 128)] = nt(px[...], got)

    issue(9, 12)
    gather(2, BLOCK)
    issue(12, 13)

    @pl.when(owns)
    def _():
        done(zred.at[pl.ds(0, NT - 1)], rr)
        over = zred[0]
        for k in range(1, NT):
            over = over + zred[k]
        tiles[index] = over.astype(HALF)

        @pl.loop(1, NT)
        def _(d):
            remote(tiles.at[index], tiles.at[index], os, og, {"table": lax.rem(t + d, NT)}).start()

    issue(13, CHUNKS)
    finish(2)
    gather(1, BLOCK)
    gather(3, BLOCK)

    @pl.when(owns)
    def _():
        done(tiles.at[pl.ds(0, OWNERS - 1)], og)

    @pl.when(jnp.logical_not(owns))
    def _():
        done(tiles, og)

    @pl.loop(1, NX)
    def _(d):
        remote(tiles, full.at[me], fs, fr, plane(lax.rem(me + d, NX))).start()

    full[me] = tiles[...]
    finish(1)
    finish(3)
    gather(0, BLOCK - 1)
    finish(0)

    done(full.at[pl.ds(0, NX - 1)], fr)
    for k in range(NX):
        for o in range(OWNERS):
            gw_ref[pl.ds(k * ROWS, ROWS), pl.ds(o * 128, 128)] = full[k, o].astype(WIDE)

    for q in range(CHUNKS - DEEP, CHUNKS):
        done(send.at[pl.ds(0, 2 if q < CHUNKS - 1 else 1)], zs.at[q])
    for q in range(4):
        done(msend.at[q, pl.ds(0, 3)], ms.at[q])
    done(part.at[pl.ds(0, F - ROWS), :], ws)
    done(full.at[pl.ds(0, NX - 1)], fs)

    @pl.when(owns)
    def _():
        done(mine.at[pl.ds(0, OWNERS - 1)], rs)
        done(zbuf.at[pl.ds(0, NT - 1), :, pl.ds(0, 128)], os)

    @pl.when(jnp.logical_not(owns))
    def _():
        done(mine, rs)


def body(pooled, upstream, lengths, w_lcb, projection, w_fmb, feature_order, col_layout):
    x = pooled.transpose(0, 2, 1).reshape(S * D, F)
    g = upstream.transpose(0, 2, 1).reshape(S * D, F)
    vmem = pl.BlockSpec(memory_space=pltpu.VMEM)
    dma = pltpu.SemaphoreType.DMA
    out, gw = pl.pallas_call(
        kernel,
        out_shape=(jax.ShapeDtypeStruct((X, 512), WIDE), jax.ShapeDtypeStruct((F, X), WIDE)),
        in_specs=[vmem] * 7 + [pl.BlockSpec(memory_space=pltpu.SMEM)],
        out_specs=(vmem, vmem),
        scratch_shapes=[
            pltpu.VMEM((S * D, F), HALF),
            pltpu.VMEM((4, X, 128), WIDE),
            pltpu.VMEM((NT, ROWS, X), HALF),
            pltpu.VMEM((NT, ROWS, X), HALF),
            pltpu.VMEM((4, 4, 32, X), HALF),
            pltpu.VMEM((4, 4, 32, X), HALF),
            pltpu.VMEM((S * D, K), HALF),
            pltpu.VMEM((S * D, K), HALF),
            pltpu.VMEM((S, K, F), HALF),
            pltpu.VMEM((F, X), WIDE),
            pltpu.VMEM((NX, ROWS, X), WIDE),
            pltpu.VMEM((OWNERS, ROWS, 128), WIDE),
            pltpu.VMEM((NT, ROWS, 128), WIDE),
            pltpu.VMEM((OWNERS, ROWS, 128), HALF),
            pltpu.VMEM((NX, OWNERS, ROWS, 128), HALF),
            pltpu.VMEM((X, X), HALF),
            dma((CHUNKS,)), dma((4,)), dma((4,)), dma((4,)),
            dma, dma, dma, dma, dma, dma, dma, dma,
        ],
        compiler_params=pltpu.CompilerParams(
            collective_id=0, has_side_effects=True, vmem_limit_bytes=48 * 1024 * 1024
        ),
        cost_estimate=pl.CostEstimate(flops=2_500_000_000, bytes_accessed=6_000_000, transcendentals=0),
        name="interaction_backward",
    )(x, g, lengths, w_lcb, projection, w_fmb, feature_order.reshape(1, F), col_layout)
    table_grads = out.reshape(ROWS, PIECE, 512).transpose(0, 2, 1)
    return table_grads, gw[:, :F], gw[:D, F + K :].T, gw[:, F : F + K].T


def solution(mesh):
    placed = P(("table", "col", "rep"), None, None)
    return jax.shard_map(
        body,
        mesh=mesh,
        in_specs=(placed, placed, P(("table", "col", "rep"), None), P(), P(), P(), P(), P()),
        out_specs=(P("table", "rep", "col"), P(), P(), P()),
        check_vma=False,
    )
```

time: 1100 us -> 136 us (0.12)
  waiting for transfers between devices: 827 us -> 0 us
  blocking collectives: 158 us -> 0 us
  Pallas kernels: 0 us -> 123 us
  starting transfers between devices: 49.9 us -> 0 us
  local copies, waits for them, and re-layouts: 31.5 us -> 10.7 us
  between operations: 14.3 us -> 0.66 us
    psum x1 -> x0, waiting for transfers between devices: 716 us -> none  [body(): summed = lax.psum((grad_lcb, grad_fmb, grad_proj), ('table', 'col', 'rep'))]
    psum x1 -> x0, blocking collectives: 158 us -> none  [body(): summed = lax.psum((grad_lcb, grad_fmb, grad_proj), ('table', 'col', 'rep'))]
    pallas_call x0 -> x1, Pallas kernels: none -> 123 us  [body(): pl.pallas_call(kernel, out_shape=(jax.ShapeDtypeStruct((X, 512), WIDE), j...]
    all_to_all x4 -> x0, waiting for transfers between devices: 111 us -> none  [the longest x1 102 us: by_group(): lax.all_to_all(bundle[0], 'table', split_axis=1, concat_axis=0, tiled=True)]
    all_to_all x4 -> x0, starting transfers between devices: 49.9 us -> none  [the longest x1 29.3 us: by_group(): lax.all_to_all(bundle[1], 'table', split_axis=1, concat_axis=0, tiled=True)]
  transfers between devices with their start and end apart: 5 -> 0, of which waited for: 3 -> 0; matrix products, arithmetic and copies ran while one was open for 3% -> 0% of each run, Pallas kernels for 0% -> 0%
where the time goes in v1:
time: 136 us; the launch traced here: 135 us
  Pallas kernels  123 us (90%)
  local copies, waits for them, and re-layouts  10.7 us (8%)
    pallas_call x1, Pallas kernels, body(): pl.pallas_call(kernel, out_shape=(jax.ShapeDtypeStruct((X, 512), WIDE), j...  123 us
    unnamed x18, local copies, waits for them, and re-layouts  9.5 us

profile of v1, /device:TPU:1, one launch (start us, length us, event | category | flops | bytes accessed | tf_op | source)
XLA Modules:
  0.0 134.7 jit_solution(1937562490374087147)
XLA Ops:
  0.6 0.8 copy.12.lay_ref
  1.4 0.0 copy-start
  1.4 1.1 copy-done
  2.5 0.0 copy-start.1
  2.5 1.1 copy-done.1
  3.6 0.0 copy-start.2
  3.6 1.0 copy-done.2
  4.6 0.0 copy-start.3
  4.6 0.8 copy-done.3
  5.5 0.0 copy-start.4
  5.5 0.8 copy-done.4
  6.2 0.0 copy-start.5
  6.2 0.7 copy-done.5
  6.9 0.0 copy-start.6
  6.9 0.7 copy-done.6
  7.6 123.4 %interaction_backward.1 = (f32[640,512]{1,0:T(8,128)S(1)}, f32[512,640]{1,0:T(8,128)S(1)}) custom-call(bf16[640,512]{1,0:T(8,128)(2,1)S(1)} %bitcast.15, bf16[640,512]{1,0:T(8,128)(2,1)S(1)} %bitcast.16, s32[4,512]{1,0:T(4,128)S(1)} %copy-done.5, bf16[512,512]{1,0:T(8,128)(2,1)S(1)} %copy-done.2, bf16[64,512]{1,0:T(8,128)(2,1)S(1)} %copy-done.3, ...), custom_call_target="tpu_custom_call" | custom-call | flops 2500000000 | bytes 6000000 | tf_op jit(solution)/shard_map/interaction_backward/pallas_call | solution.py:285
  131.0 0.1 slice_bitcast_fusion.1
  131.0 0.7 copy.13
  131.8 1.1 slice.9
  132.9 0.8 copy.14
  133.7 1.1 copy.16
  (1 shorter events, 0.0 us)
Async XLA Ops:
  1.4 1.1 copy-start
  2.5 1.1 copy-start.1
  3.6 1.0 copy-start.2
  4.6 0.8 copy-start.3
  5.5 0.8 copy-start.4
  6.2 0.7 copy-start.5
  6.9 0.7 copy-start.6

commit v2 on v1

v2 whole, which is shorter than its diff:
```python
import jax
import jax.numpy as jnp
from jax import lax
from jax.experimental import pallas as pl
from jax.experimental.pallas import tpu as pltpu
from jax.sharding import PartitionSpec as P

MESH = pl.DeviceIdType.MESH
WIDE = jnp.float32
HALF = jnp.bfloat16
S = 4
F = 512
D = 160
K = 64
PIECE = 40
ROWS = 16
X = 640
NT = 32
NX = 32
BATCH = 8
OWNERS = 5
APART = 7
RUN = 4


def nn(a, b):
    return lax.dot_general(a, b, (((1,), (0,)), ((), ())), preferred_element_type=WIDE)


def nt(a, b):
    return lax.dot_general(a, b, (((1,), (1,)), ((), ())), preferred_element_type=WIDE)


def tn(a, b):
    return lax.dot_general(a, b, (((0,), (0,)), ((), ())), preferred_element_type=WIDE)


def one_hot(mask):
    return jnp.where(mask, 1.0, 0.0).astype(HALF)


def iota(shape, dim):
    return lax.broadcasted_iota(jnp.int32, shape, dim)


def kernel(
    x_hbm, g_hbm, len_hbm, lcb_hbm, proj_hbm, fmb_hbm, order_hbm, lay_ref,
    rows_ref, full,
    x_ref, g_ref, len_ref, lcb_ref, proj_ref, fmb_ref, order_ref,
    rst, wide, send, zbuf, msend, mrecv, ct, gct, git, part, pbuf, wbuf, mine, zred, tiles,
    ins, zs, zr, ms, mr, ps, pr, ws, wr, rs, rr, os, og, hs, fs, fr,
):
    t = lax.axis_index("table")
    c = lax.axis_index("col")
    r = lax.axis_index("rep")
    me = c * 8 + r

    def plane(k):
        return {"col": k // 8, "rep": lax.rem(k, 8)}

    def remote(src, dst, ss, rsem, device):
        return pltpu.make_async_remote_copy(
            src_ref=src, dst_ref=dst, send_sem=ss, recv_sem=rsem, device_id=device, device_id_type=MESH
        )

    def done(ref, sem):
        pltpu.make_async_copy(ref, ref, sem).wait()

    arriving = [
        pltpu.make_async_copy(src, dst, ins.at[n])
        for n, (src, dst) in enumerate((
            (g_hbm, g_ref), (fmb_hbm, fmb_ref), (x_hbm, x_ref), (proj_hbm, proj_ref),
            (lcb_hbm, lcb_ref), (len_hbm, len_ref), (order_hbm, order_ref),
        ))
    ]
    for copy in arriving:
        copy.start()

    barrier = pltpu.get_barrier_semaphore()

    @pl.loop(1, NT)
    def _(d):
        pl.semaphore_signal(barrier, inc=1, device_id={"table": lax.rem(t + d, NT)}, device_id_type=MESH)

    @pl.loop(1, NX)
    def _(d):
        pl.semaphore_signal(barrier, inc=1, device_id=plane(lax.rem(me + d, NX)), device_id_type=MESH)

    for copy in arriving:
        copy.wait()

    proj = proj_ref[...]
    ct[...] = nt(x_ref[...], proj).astype(HALF)
    for i in range(S):
        rows = pl.ds(i * D, D)
        git[i] = nn(fmb_ref[...], g_ref[rows, :]).astype(HALF)
        gct[rows, :] = nt(x_ref[rows, :], git[i]).astype(HALF)
    for i in range(S):
        rows = pl.ds(i * D, D)
        g = g_ref[rows, :]
        grad = g.astype(WIDE) + nn(g, lcb_ref[...])
        grad = grad + nn(ct[rows, :], git[i])
        grad = grad + nn(gct[rows, :], proj)
        averaged = grad * (1.0 / len_ref[pl.ds(i, 1), :].astype(WIDE))
        largest = jnp.max(jnp.abs(averaged), axis=0, keepdims=True)
        scale = (largest + 1e-06).astype(HALF).astype(WIDE)
        quantized = (averaged * (1.0 / scale)).astype(HALF)
        rst[rows, :] = (quantized.astype(WIDE) * scale).astype(HALF)

    into = one_hot(iota((F, F), 0) == order_ref[...])
    for i in range(S):
        ordered = nn(rst[pl.ds(i * D, D), :], into)
        for j in range(4):
            for gb in range(4):
                wide[gb, pl.ds(i * 4 + j, PIECE, stride=ROWS), :] = ordered[
                    j * PIECE : (j + 1) * PIECE, gb * 128 : (gb + 1) * 128
                ]

    lane_block = iota((ROWS, 128), 1) // 16
    for eb in range(5):
        for gb in range(4):
            turned = []
            for e in range(8):
                tile = wide[gb, pl.ds((eb * 8 + e) * ROWS, ROWS), :]
                turned.append(pltpu.roll(tile, 16 * e, 1) if e else tile)
            for g in range(8):
                mixed = turned[0]
                for e in range(1, 8):
                    mixed = jnp.where(lane_block == (g + e) % 8, turned[e], mixed)
                send[gb * 8 + g, :, pl.ds(eb * 128, 128)] = mixed.astype(HALF)
    zbuf[t] = send[t]

    def distance(m):
        return (30 - m) // 2 + 1

    waited = [0]

    def issue(first, last, deep):
        def left(m):
            done(send.at[0], zs.at[m])

        early = max(waited[0], first - deep)
        pl.loop(waited[0], early)(left)

        @pl.loop(first, last)
        def _(m):
            pl.when(m >= early + deep)(lambda: left(m - deep))
            d = distance(m)
            p = lax.rem(t + jnp.where(lax.rem(m, 2) == 0, d, NT - d), NT)
            remote(send.at[p], zbuf.at[t], zs.at[m], zr.at[(m + 1) // BATCH], {"table": p}).start()

        waited[0] = max(early, last - deep)

    def source(n, u):
        low, high = (13, 20) if n == 0 else (13 - 4 * n, 17 - 4 * n)
        if n == 0:
            offset = 0 if u == 7 else 13 + u
        else:
            offset = low + u if u < 4 else NT - low - (u - 4)
        return lax.rem(t + offset, NT)


    fmb_part = jnp.zeros((D, K), WIDE)
    for i in range(S):
        rows = pl.ds(i * D, D)
        interact = tn(ct[rows, :], x_ref[rows, :]).astype(HALF)
        fmb_part = fmb_part + nt(g_ref[rows, :], interact)
    part[:, pl.ds(0, F)] = tn(g_ref[...], x_ref[...])
    proj_part = tn(x_ref[...], gct[...])
    pad = jnp.zeros((F - D, K), WIDE)
    part[:, pl.ds(F, 128)] = jnp.concatenate([proj_part, jnp.concatenate([fmb_part, pad], axis=0)], axis=1)

    pl.semaphore_wait(barrier, NT + NX - 2)
    issue(0, 9, 9)

    core = lax.rem(c, 2)
    for u in range(2):
        rows = pl.ds(pl.multiple_of((1 - core + 2 * u) * 128, 128), 128)
        remote(part.at[rows, :], pbuf.at[u], ps, pr, {"col": c + 1 - 2 * core}).start()

    def pair_sum():
        done(pbuf, pr)
        for u in range(2):
            rows = pl.ds(pl.multiple_of((core + 2 * u) * 128, 128), 128)
            part[rows, :] = part[rows, :] + pbuf[u]
        at = (c // 2) * 8 + r

        @pl.loop(1, NX // 2)
        def _(d):
            w = lax.rem(at + d, NX // 2)
            k = (core + 2 * (w // 8)) * 8 + lax.rem(w, 8)
            rows = pl.ds(pl.multiple_of(k * ROWS, ROWS), ROWS)
            remote(part.at[rows, :], wbuf.at[at], ws, wr, plane(k)).start()

        wbuf[at] = part[pl.ds(pl.multiple_of(me * ROWS, ROWS), ROWS), :]

    a = iota((128, 128), 0)
    b = iota((128, 128), 1)
    j = b % 4
    owner = jnp.where(
        j == 0, lay_ref[0, t], jnp.where(j == 1, lay_ref[1, t], jnp.where(j == 2, lay_ref[2, t], lay_ref[3, t]))
    )
    by_column = one_hot((a % 32 == b // 4) & (owner == a // 32))
    by_sample = one_hot(b == ((a // 4) % 4) * 32 + (a // 16) * 4 + a % 4)

    def gather(n):
        done(zbuf.at[pl.ds(0, 8 if n else 7)], zr.at[n])
        got = jnp.concatenate([zbuf[source(n, u)] for u in range(BATCH)], axis=0)
        msend[n] = nn(by_column, got).astype(HALF).reshape(4, 32, X)
        for d in range(1, 4):
            k = lax.rem(c + d, 4)
            remote(msend.at[n, k], mrecv.at[n, c], ms.at[n], mr.at[n], {"col": k}).start()
        mrecv[n, c] = msend[n, c]

    def finish(n):
        done(mrecv.at[n, pl.ds(0, 3)], mr.at[n])
        got = nn(by_sample, mrecv[n].reshape(128, X)).astype(HALF)
        for u in range(BATCH):
            rows_ref[source(n, u)] = got[u * ROWS : (u + 1) * ROWS, :]

    turn = lax.rem(t - me + NT, NT)
    owns = (lax.rem(turn, APART) == 0) & (turn < OWNERS * APART)
    index = jnp.minimum(turn // APART, OWNERS - 1)

    def plane_sum():
        done(wbuf.at[pl.ds(0, NX // 2 - 1)], wr)
        total = wbuf[0]
        for k in range(1, NX // 2):
            total = total + wbuf[k]
        for o in range(OWNERS):
            mine[o] = total[:, o * 128 : (o + 1) * 128]
        for o in range(OWNERS):
            to = lax.rem(me + o * APART, NT)

            @pl.when(to != t)
            def _():
                remote(mine.at[o], zred.at[t], rs, rr, {"table": to}).start()

        zred[t] = mine[index]

    def table_sum():
        @pl.when(owns)
        def _():
            done(zred.at[pl.ds(0, NT - 1)], rr)
            over = zred[0]
            for k in range(1, NT):
                over = over + zred[k]
            tiles[index] = over.astype(HALF)

            @pl.loop(1, NT // RUN + RUN - 1)
            def _(d):
                to = jnp.where(d < NT // RUN, d * RUN, d - NT // RUN + 1)
                remote(tiles.at[index], tiles.at[index], os, og.at[index], {"table": lax.rem(t + to, NT)}).start()

    def behind(o):
        return lax.rem(turn - o * APART + NT, NT)

    def first(o):
        return (lax.rem(behind(o), RUN) == 0) & (behind(o) > 0)

    def hand_on():
        for o in range(OWNERS):

            @pl.when(first(o))
            def _():
                done(tiles.at[o], og.at[o])
                for d in range(1, RUN):
                    remote(tiles.at[o], tiles.at[o], hs.at[o], og.at[o], {"table": lax.rem(t + d, NT)}).start()

    def round_plane():
        for o in range(OWNERS):

            @pl.when(lax.rem(behind(o), RUN) > 0)
            def _():
                done(tiles.at[o], og.at[o])

        @pl.loop(1, NX)
        def _(d):
            remote(tiles, full.at[me], fs, fr, plane(lax.rem(me + d, NX))).start()

        full[me] = tiles[...]

    pair_sum()
    plane_sum()
    issue(9, 18, 9)
    gather(0)
    table_sum()
    issue(18, 24, 7)
    finish(0)
    gather(1)
    hand_on()
    issue(24, 31, 6)
    finish(1)
    round_plane()
    gather(2)
    finish(2)
    gather(3)
    finish(3)

    done(full.at[pl.ds(0, NX - 1)], fr)
    for m in range(waited[0], 31):
        done(send.at[0], zs.at[m])
    for n in range(4):
        done(msend.at[n, pl.ds(0, 3)], ms.at[n])
    done(pbuf, ps)
    done(part.at[pl.ds(0, F // 2 - ROWS), :], ws)
    done(full.at[pl.ds(0, NX - 1)], fs)

    @pl.when(owns)
    def _():
        done(mine.at[pl.ds(0, OWNERS - 1)], rs)
        done(zbuf.at[pl.ds(0, NT // RUN + RUN - 2), :, pl.ds(0, 128)], os)

    @pl.when(jnp.logical_not(owns))
    def _():
        done(mine, rs)

    for o in range(OWNERS):

        @pl.when(first(o))
        def _():
            done(tiles.at[pl.ds(0, RUN - 1)], hs.at[o])


def place(rows_ref, full, out_ref, lcb_ref, fmb_ref, proj_ref):
    t = lax.axis_index("table")
    e = iota((PIECE, X), 0)
    spot = (e // 8) * 128 + lax.rem(lax.rem(e, 8) + lax.rem(t, 8), 8) * 16
    px = jnp.concatenate([one_hot(iota((PIECE, X), 1) == spot + h) for h in range(ROWS)], axis=0)
    out_ref[...] = nt(px, rows_ref[...])
    tail = []
    for k in range(NX):
        rows = pl.ds(k * ROWS, ROWS)
        for o in range(4):
            lcb_ref[rows, pl.ds(o * 128, 128)] = full[k, o].astype(WIDE)
        tail.append(full[k, 4].astype(WIDE))
    tail = jnp.concatenate(tail, axis=0).T
    proj_ref[...] = tail[:K, :]
    fmb_ref[...] = tail[K:, :D]


def body(pooled, upstream, lengths, w_lcb, projection, w_fmb, feature_order, col_layout):
    x = pooled.transpose(0, 2, 1).reshape(S * D, F)
    g = upstream.transpose(0, 2, 1).reshape(S * D, F)
    vmem = pl.BlockSpec(memory_space=pltpu.VMEM)
    hbm = pl.BlockSpec(memory_space=pl.ANY)
    dma = pltpu.SemaphoreType.DMA
    rows, full = pl.pallas_call(
        kernel,
        out_shape=(
            jax.ShapeDtypeStruct((NT, ROWS, X), HALF),
            jax.ShapeDtypeStruct((NX, OWNERS, ROWS, 128), HALF),
        ),
        in_specs=[hbm] * 7 + [pl.BlockSpec(memory_space=pltpu.SMEM)],
        out_specs=(vmem, vmem),
        scratch_shapes=[
            pltpu.VMEM((S * D, F), HALF),
            pltpu.VMEM((S * D, F), HALF),
            pltpu.VMEM((S, F), jnp.int32),
            pltpu.VMEM((F, F), HALF),
            pltpu.VMEM((K, F), HALF),
            pltpu.VMEM((K, D), HALF),
            pltpu.VMEM((1, F), jnp.int32),
            pltpu.VMEM((S * D, F), HALF),
            pltpu.VMEM((4, X, 128), WIDE),
            pltpu.VMEM((NT, ROWS, X), HALF),
            pltpu.VMEM((NT, ROWS, X), HALF),
            pltpu.VMEM((4, 4, 32, X), HALF),
            pltpu.VMEM((4, 4, 32, X), HALF),
            pltpu.VMEM((S * D, K), HALF),
            pltpu.VMEM((S * D, K), HALF),
            pltpu.VMEM((S, K, F), HALF),
            pltpu.VMEM((F, X), WIDE),
            pltpu.VMEM((2, 128, X), WIDE),
            pltpu.VMEM((NX // 2, ROWS, X), WIDE),
            pltpu.VMEM((OWNERS, ROWS, 128), WIDE),
            pltpu.VMEM((NT, ROWS, 128), WIDE),
            pltpu.VMEM((OWNERS, ROWS, 128), HALF),
            dma((7,)), dma((31,)), dma((4,)), dma((4,)), dma((4,)),
            dma, dma, dma, dma, dma, dma, dma, dma((OWNERS,)), dma((OWNERS,)), dma, dma,
        ],
        compiler_params=pltpu.CompilerParams(
            collective_id=0, has_side_effects=True, vmem_limit_bytes=56 * 1024 * 1024
        ),
        cost_estimate=pl.CostEstimate(flops=2_500_000_000, bytes_accessed=6_000_000, transcendentals=0),
        name="interaction_backward",
    )(x, g, lengths, w_lcb, projection, w_fmb, feature_order.reshape(1, F), col_layout.T)
    out, lcb, fmb, proj = pl.pallas_call(
        place,
        out_shape=(
            jax.ShapeDtypeStruct((X, 512), WIDE),
            jax.ShapeDtypeStruct((F, F), WIDE),
            jax.ShapeDtypeStruct((K, D), WIDE),
            jax.ShapeDtypeStruct((K, F), WIDE),
        ),
        in_specs=[vmem] * 2,
        out_specs=(vmem,) * 4,
        compiler_params=pltpu.CompilerParams(vmem_limit_bytes=32 * 1024 * 1024),
        name="place",
    )(rows.reshape(512, X), full)
    return out.reshape(ROWS, PIECE, 512).transpose(0, 2, 1), lcb, fmb, proj


def solution(mesh):
    placed = P(("table", "col", "rep"), None, None)
    return jax.shard_map(
        body,
        mesh=mesh,
        in_specs=(placed, placed, P(("table", "col", "rep"), None), P(), P(), P(), P(), P()),
        out_specs=(P("table", "rep", "col"), P(), P(), P()),
        check_vma=False,
    )
```

time: 136 us -> 114 us (0.84)
  Pallas kernels: 123 us -> 110 us
  local copies, waits for them, and re-layouts: 10.7 us -> 2.17 us
    pallas_call x1 -> x2, Pallas kernels: 123 us -> 110 us  [the longest x1 108 us: body(): pl.pallas_call(kernel, out_shape=(jax.ShapeDtypeStruct((NT, ROWS, X), HAL...]
    unnamed x18 -> x4, local copies, waits for them, and re-layouts: 9.5 us -> 2.17 us
where the time goes in v2:
time: 114 us; the launch traced here: 113 us
  Pallas kernels  110 us (96%)
  local copies, waits for them, and re-layouts  2.17 us (2%)
    pallas_call x1, Pallas kernels, body(): pl.pallas_call(kernel, out_shape=(jax.ShapeDtypeStruct((NT, ROWS, X), HAL...  108 us

profile of v2, /device:TPU:1, one launch (start us, length us, event | category | flops | bytes accessed | tf_op | source)
XLA Modules:
  0.0 113.3 jit_solution(7189999033683518282)
XLA Ops:
  0.6 108.3 %interaction_backward.1 = (bf16[32,16,640]{2,1,0:T(8,128)(2,1)}, bf16[32,5,16,128]{3,2,1,0:T(8,128)(2,1)}) custom-call(bf16[640,512]{1,0:T(8,128)(2,1)} %bitcast.14, bf16[640,512]{1,0:T(8,128)(2,1)} %bitcast.15, s32[4,512]{1,0:T(4,128)} %len_hbm.1, bf16[512,512]{1,0:T(8,128)(2,1)} %lcb_hbm.1, bf16[64,512]{1,0:T(8,128)(2,1)} %proj_hbm.1, ...), custom_call_target="tpu_custom_call" | custom-call | flops 2500000000 | bytes 6000000 | tf_op jit(solution)/shard_map/interaction_backward/pallas_call | solution.py:348
  108.9 0.0 copy-start
  109.0 1.1 copy-done
  110.0 0.0 copy-start.1
  110.0 1.1 copy-done.1
  111.1 2.2 %place.1 = (f32[640,512]{1,0:T(8,128)}, f32[512,512]{1,0:T(8,128)}, f32[64,160]{1,0:T(8,128)}, f32[64,512]{1,0:T(8,128)}) custom-call(bf16[512,640]{1,0:T(8,128)(2,1)S(1)} %bitcast.12, bf16[32,5,16,128]{3,2,1,0:T(8,128)(2,1)S(1)} %copy-done.1), custom_call_target="tpu_custom_call" | custom-call | tf_op jit(solution)/shard_map/place/pallas_call | solution.py:388
Async XLA Ops:
  108.9 1.1 copy-start
  110.0 1.1 copy-start.1

commit v3 on v2

--- a/solution.py
+++ b/solution.py
@@ -17,7 +17,7 @@
 X = 640
 NT = 32
 NX = 32
-BATCH = 8
+BATCH = (8, 8, 8, 4, 4)
 OWNERS = 5
 APART = 7
 RUN = 4
@@ -147,18 +147,18 @@
             pl.when(m >= early + deep)(lambda: left(m - deep))
             d = distance(m)
             p = lax.rem(t + jnp.where(lax.rem(m, 2) == 0, d, NT - d), NT)
-            remote(send.at[p], zbuf.at[t], zs.at[m], zr.at[(m + 1) // BATCH], {"table": p}).start()
+            remote(send.at[p], zbuf.at[t], zs.at[m], zr.at[(m + 1) // 8 + m // 27], {"table": p}).start()
 
         waited[0] = max(early, last - deep)
 
     def source(n, u):
-        low, high = (13, 20) if n == 0 else (13 - 4 * n, 17 - 4 * n)
         if n == 0:
             offset = 0 if u == 7 else 13 + u
         else:
-            offset = low + u if u < 4 else NT - low - (u - 4)
+            low = (13, 9, 5, 3, 1)[n]
+            half = BATCH[n] // 2
+            offset = low + u if u < half else NT - low - (u - half)
         return lax.rem(t + offset, NT)
-
 
     fmb_part = jnp.zeros((D, K), WIDE)
     for i in range(S):
@@ -194,28 +194,38 @@
 
         wbuf[at] = part[pl.ds(pl.multiple_of(me * ROWS, ROWS), ROWS), :]
 
-    a = iota((128, 128), 0)
-    b = iota((128, 128), 1)
-    j = b % 4
-    owner = jnp.where(
-        j == 0, lay_ref[0, t], jnp.where(j == 1, lay_ref[1, t], jnp.where(j == 2, lay_ref[2, t], lay_ref[3, t]))
-    )
-    by_column = one_hot((a % 32 == b // 4) & (owner == a // 32))
-    by_sample = one_hot(b == ((a // 4) % 4) * 32 + (a // 16) * 4 + a % 4)
+    def orders(size):
+        a = iota((16 * size, 16 * size), 0)
+        b = iota((16 * size, 16 * size), 1)
+        j = b % 4
+        owner = jnp.where(
+            j == 0, lay_ref[0, t], jnp.where(j == 1, lay_ref[1, t], jnp.where(j == 2, lay_ref[2, t], lay_ref[3, t]))
+        )
+        by_column = one_hot((a % (4 * size) == b // 4) & (owner == a // (4 * size)))
+        by_sample = one_hot(b == ((a // 4) % 4) * (4 * size) + (a // 16) * 4 + a % 4)
+        return by_column, by_sample
+
+    order = {size: orders(size) for size in sorted(set(BATCH))}
 
     def gather(n):
-        done(zbuf.at[pl.ds(0, 8 if n else 7)], zr.at[n])
-        got = jnp.concatenate([zbuf[source(n, u)] for u in range(BATCH)], axis=0)
-        msend[n] = nn(by_column, got).astype(HALF).reshape(4, 32, X)
+        size = BATCH[n]
+        part_rows = pl.ds(0, 4 * size)
+        done(zbuf.at[pl.ds(0, size if n else size - 1)], zr.at[n])
+        got = jnp.concatenate([zbuf[source(n, u)] for u in range(size)], axis=0)
+        msend[n, :, part_rows, :] = nn(order[size][0], got).astype(HALF).reshape(4, 4 * size, X)
         for d in range(1, 4):
             k = lax.rem(c + d, 4)
-            remote(msend.at[n, k], mrecv.at[n, c], ms.at[n], mr.at[n], {"col": k}).start()
-        mrecv[n, c] = msend[n, c]
+            remote(
+                msend.at[n, k, part_rows, :], mrecv.at[n, c, part_rows, :], ms.at[n], mr.at[n], {"col": k}
+            ).start()
+        mrecv[n, c, part_rows, :] = msend[n, c, part_rows, :]
 
     def finish(n):
-        done(mrecv.at[n, pl.ds(0, 3)], mr.at[n])
-        got = nn(by_sample, mrecv[n].reshape(128, X)).astype(HALF)
-        for u in range(BATCH):
+        size = BATCH[n]
+        part_rows = pl.ds(0, 4 * size)
+        done(mrecv.at[n, pl.ds(0, 3), part_rows, :], mr.at[n])
+        got = nn(order[size][1], mrecv[n, :, part_rows, :].reshape(16 * size, X)).astype(HALF)
+        for u in range(size):
             rows_ref[source(n, u)] = got[u * ROWS : (u + 1) * ROWS, :]
 
     turn = lax.rem(t - me + NT, NT)
@@ -228,7 +238,7 @@
         for k in range(1, NX // 2):
             total = total + wbuf[k]
         for o in range(OWNERS):
-            mine[o] = total[:, o * 128 : (o + 1) * 128]
+            mine[o] = total[:, o * 128 : (o + 1) * 128].astype(HALF)
         for o in range(OWNERS):
             to = lax.rem(me + o * APART, NT)
 
@@ -242,9 +252,9 @@
         @pl.when(owns)
         def _():
             done(zred.at[pl.ds(0, NT - 1)], rr)
-            over = zred[0]
+            over = zred[0].astype(WIDE)
             for k in range(1, NT):
-                over = over + zred[k]
+                over = over + zred[k].astype(WIDE)
             tiles[index] = over.astype(HALF)
 
             @pl.loop(1, NT // RUN + RUN - 1)
@@ -282,26 +292,27 @@
 
     pair_sum()
     plane_sum()
-    issue(9, 18, 9)
+    issue(9, 20, 12)
     gather(0)
     table_sum()
-    issue(18, 24, 7)
+    issue(20, 31, 12)
     finish(0)
     gather(1)
     hand_on()
-    issue(24, 31, 6)
     finish(1)
+    gather(2)
     round_plane()
-    gather(2)
     finish(2)
     gather(3)
     finish(3)
+    gather(4)
+    finish(4)
 
     done(full.at[pl.ds(0, NX - 1)], fr)
     for m in range(waited[0], 31):
         done(send.at[0], zs.at[m])
-    for n in range(4):
-        done(msend.at[n, pl.ds(0, 3)], ms.at[n])
+    for n, size in enumerate(BATCH):
+        done(msend.at[n, pl.ds(0, 3), pl.ds(0, 4 * size), :], ms.at[n])
     done(pbuf, ps)
     done(part.at[pl.ds(0, F // 2 - ROWS), :], ws)
     done(full.at[pl.ds(0, NX - 1)], fs)
@@ -322,21 +333,39 @@
             done(tiles.at[pl.ds(0, RUN - 1)], hs.at[o])
 
 
-def place(rows_ref, full, out_ref, lcb_ref, fmb_ref, proj_ref):
+def place(rows_hbm, full_hbm, out_hbm, lcb_hbm, fmb_hbm, proj_hbm, rows, full, out, lcb, fmb, proj, ins, outs):
+    fetch = [
+        pltpu.make_async_copy(src, dst, ins.at[n])
+        for n, (src, dst) in enumerate(((rows_hbm, rows), (full_hbm, full)))
+    ]
+    store = [
+        pltpu.make_async_copy(src, dst, outs.at[n])
+        for n, (src, dst) in enumerate(((out, out_hbm), (lcb, lcb_hbm), (fmb, fmb_hbm), (proj, proj_hbm)))
+    ]
+    for copy in fetch:
+        copy.start()
     t = lax.axis_index("table")
     e = iota((PIECE, X), 0)
     spot = (e // 8) * 128 + lax.rem(lax.rem(e, 8) + lax.rem(t, 8), 8) * 16
     px = jnp.concatenate([one_hot(iota((PIECE, X), 1) == spot + h) for h in range(ROWS)], axis=0)
-    out_ref[...] = nt(px, rows_ref[...])
+    fetch[0].wait()
+    out[...] = nt(px, rows[...])
+    store[0].start()
+    fetch[1].wait()
     tail = []
     for k in range(NX):
-        rows = pl.ds(k * ROWS, ROWS)
+        at = pl.ds(k * ROWS, ROWS)
         for o in range(4):
-            lcb_ref[rows, pl.ds(o * 128, 128)] = full[k, o].astype(WIDE)
+            lcb[at, pl.ds(o * 128, 128)] = full[k, o].astype(WIDE)
         tail.append(full[k, 4].astype(WIDE))
+    store[1].start()
     tail = jnp.concatenate(tail, axis=0).T
-    proj_ref[...] = tail[:K, :]
-    fmb_ref[...] = tail[K:, :D]
+    proj[...] = tail[:K, :]
+    fmb[...] = tail[K:, :D]
+    store[2].start()
+    store[3].start()
+    for copy in store:
+        copy.wait()
 
 
 def body(pooled, upstream, lengths, w_lcb, projection, w_fmb, feature_order, col_layout):
@@ -365,18 +394,18 @@
             pltpu.VMEM((4, X, 128), WIDE),
             pltpu.VMEM((NT, ROWS, X), HALF),
             pltpu.VMEM((NT, ROWS, X), HALF),
-            pltpu.VMEM((4, 4, 32, X), HALF),
-            pltpu.VMEM((4, 4, 32, X), HALF),
+            pltpu.VMEM((len(BATCH), 4, 32, X), HALF),
+            pltpu.VMEM((len(BATCH), 4, 32, X), HALF),
             pltpu.VMEM((S * D, K), HALF),
             pltpu.VMEM((S * D, K), HALF),
             pltpu.VMEM((S, K, F), HALF),
             pltpu.VMEM((F, X), WIDE),
             pltpu.VMEM((2, 128, X), WIDE),
             pltpu.VMEM((NX // 2, ROWS, X), WIDE),
-            pltpu.VMEM((OWNERS, ROWS, 128), WIDE),
-            pltpu.VMEM((NT, ROWS, 128), WIDE),
             pltpu.VMEM((OWNERS, ROWS, 128), HALF),
-            dma((7,)), dma((31,)), dma((4,)), dma((4,)), dma((4,)),
+            pltpu.VMEM((NT, ROWS, 128), HALF),
+            pltpu.VMEM((OWNERS, ROWS, 128), HALF),
+            dma((7,)), dma((31,)), dma((len(BATCH),)), dma((len(BATCH),)), dma((len(BATCH),)),
             dma, dma, dma, dma, dma, dma, dma, dma((OWNERS,)), dma((OWNERS,)), dma, dma,
         ],
         compiler_params=pltpu.CompilerParams(
@@ -393,9 +422,18 @@
             jax.ShapeDtypeStruct((K, D), WIDE),
             jax.ShapeDtypeStruct((K, F), WIDE),
         ),
-        in_specs=[vmem] * 2,
-        out_specs=(vmem,) * 4,
-        compiler_params=pltpu.CompilerParams(vmem_limit_bytes=32 * 1024 * 1024),
+        in_specs=[hbm] * 2,
+        out_specs=(hbm,) * 4,
+        scratch_shapes=[
+            pltpu.VMEM((512, X), HALF),
+            pltpu.VMEM((NX, OWNERS, ROWS, 128), HALF),
+            pltpu.VMEM((X, 512), WIDE),
+            pltpu.VMEM((F, F), WIDE),
+            pltpu.VMEM((K, D), WIDE),
+            pltpu.VMEM((K, F), WIDE),
+            dma((2,)), dma((4,)),
+        ],
+        compiler_params=pltpu.CompilerParams(vmem_limit_bytes=56 * 1024 * 1024),
         name="place",
     )(rows.reshape(512, X), full)
     return out.reshape(ROWS, PIECE, 512).transpose(0, 2, 1), lcb, fmb, proj

time: 114 us -> 110 us (0.965)
  local copies, waits for them, and re-layouts: 2.17 us -> 0 us
    pallas_call x1, Pallas kernels: 108 us -> 106 us  [body(): pl.pallas_call(kernel, out_shape=(jax.ShapeDtypeStruct((NT, ROWS, X), HAL...]
    unnamed x4 -> x0, local copies, waits for them, and re-layouts: 2.17 us -> none
    pallas_call x1, Pallas kernels: 2.15 us -> 3.3 us  [body(): pl.pallas_call(place, out_shape=(jax.ShapeDtypeStruct((X, 512), WIDE), ja...]
where the time goes in v3:
time: 110 us
  Pallas kernels  109 us (99%)
    pallas_call x1, Pallas kernels, body(): pl.pallas_call(kernel, out_shape=(jax.ShapeDtypeStruct((NT, ROWS, X), HAL...  106 us
    pallas_call x1, Pallas kernels, body(): pl.pallas_call(place, out_shape=(jax.ShapeDtypeStruct((X, 512), WIDE), ja...  3.3 us

profile of v3, /device:TPU:1, one launch (start us, length us, event | category | flops | bytes accessed | tf_op | source)
XLA Modules:
  0.0 109.6 jit_solution(12498864028513820469)
XLA Ops:
  0.6 105.7 %interaction_backward.1 = (bf16[32,16,640]{2,1,0:T(8,128)(2,1)}, bf16[32,5,16,128]{3,2,1,0:T(8,128)(2,1)}) custom-call(bf16[640,512]{1,0:T(8,128)(2,1)} %bitcast.14, bf16[640,512]{1,0:T(8,128)(2,1)} %bitcast.15, s32[4,512]{1,0:T(4,128)} %len_hbm.1, bf16[512,512]{1,0:T(8,128)(2,1)} %lcb_hbm.1, bf16[64,512]{1,0:T(8,128)(2,1)} %proj_hbm.1, ...), custom_call_target="tpu_custom_call" | custom-call | flops 2500000000 | bytes 6000000 | tf_op jit(solution)/shard_map/interaction_backward/pallas_call | solution.py:377
  106.3 3.3 %place.1 = (f32[640,512]{1,0:T(8,128)}, f32[512,512]{1,0:T(8,128)}, f32[64,160]{1,0:T(8,128)}, f32[64,512]{1,0:T(8,128)}) custom-call(bf16[512,640]{1,0:T(8,128)(2,1)} %bitcast.12, bf16[32,5,16,128]{3,2,1,0:T(8,128)(2,1)} %get-tuple-element.11.full_hbm), custom_call_target="tpu_custom_call" | custom-call | tf_op jit(solution)/shard_map/place/pallas_call | solution.py:417

commit v4 on v3

--- a/solution.py
+++ b/solution.py
@@ -171,7 +171,7 @@
     part[:, pl.ds(F, 128)] = jnp.concatenate([proj_part, jnp.concatenate([fmb_part, pad], axis=0)], axis=1)
 
     pl.semaphore_wait(barrier, NT + NX - 2)
-    issue(0, 9, 9)
+    issue(0, 7, 7)
 
     core = lax.rem(c, 2)
     for u in range(2):
@@ -292,10 +292,10 @@
 
     pair_sum()
     plane_sum()
-    issue(9, 20, 12)
+    issue(7, 17, 12)
     gather(0)
     table_sum()
-    issue(20, 31, 12)
+    issue(17, 31, 10)
     finish(0)
     gather(1)
     hand_on()

time: 110 us -> 110 us (level)
  no operation moved by 1% of the time
where the time goes in v4:
time: 110 us; the launch traced here: 109 us
  Pallas kernels  108 us (98%)
    pallas_call x1, Pallas kernels, body(): pl.pallas_call(kernel, out_shape=(jax.ShapeDtypeStruct((NT, ROWS, X), HAL...  105 us
    pallas_call x1, Pallas kernels, body(): pl.pallas_call(place, out_shape=(jax.ShapeDtypeStruct((X, 512), WIDE), ja...  3.3 us

profile of v4, /device:TPU:1, one launch (start us, length us, event | category | flops | bytes accessed | tf_op | source)
XLA Modules:
  0.0 108.9 jit_solution(8178221866192927511)
XLA Ops:
  0.6 105.0 %interaction_backward.1 = (bf16[32,16,640]{2,1,0:T(8,128)(2,1)}, bf16[32,5,16,128]{3,2,1,0:T(8,128)(2,1)}) custom-call(bf16[640,512]{1,0:T(8,128)(2,1)} %bitcast.14, bf16[640,512]{1,0:T(8,128)(2,1)} %bitcast.15, s32[4,512]{1,0:T(4,128)} %len_hbm.1, bf16[512,512]{1,0:T(8,128)(2,1)} %lcb_hbm.1, bf16[64,512]{1,0:T(8,128)(2,1)} %proj_hbm.1, ...), custom_call_target="tpu_custom_call" | custom-call | flops 2500000000 | bytes 6000000 | tf_op jit(solution)/shard_map/interaction_backward/pallas_call | solution.py:377
  105.6 3.3 %place.1 = (f32[640,512]{1,0:T(8,128)}, f32[512,512]{1,0:T(8,128)}, f32[64,160]{1,0:T(8,128)}, f32[64,512]{1,0:T(8,128)}) custom-call(bf16[512,640]{1,0:T(8,128)(2,1)} %bitcast.12, bf16[32,5,16,128]{3,2,1,0:T(8,128)(2,1)} %get-tuple-element.11.full_hbm), custom_call_target="tpu_custom_call" | custom-call | tf_op jit(solution)/shard_map/place/pallas_call | solution.py:417
